TPU v7x, 32 devices: a whole 2x2x4 slice. The times are simulated.
32 devices in a mesh: dp: 8 (over z, y), mp: 4 (over x, core).
Axes of the slice: x: 2, y: 2, z: 4, core: 2. Of those that a mesh axis runs over, the one named last changes fastest.
Arguments:
- tokens: bfloat16 [14336, 1024], P('dp'), may hold values from -60 to 60
- segment_ids: int32 [14336], P('dp'), may hold values from 0 to 31, as said below
- page_table: int32 [112], P('dp'), may hold values from 0 to 111, as said below
- w_query: bfloat16 [1024, 1024], P('dp', 'mp'), may hold values from -0.1875 to 0.1875
- w_key: bfloat16 [1024, 1024], P('dp', 'mp'), may hold values from -0.1875 to 0.1875
- w_value: bfloat16 [1024, 1024], P('dp', 'mp'), may hold values from -0.1875 to 0.1875
- w_out: bfloat16 [1024, 1024], P('mp', 'dp'), may hold values from -1.5 to 1.5
- w_up: bfloat16 [1024, 4096], P('dp', 'mp'), may hold values from -0.1875 to 0.1875
- w_down: bfloat16 [4096, 1024], P('mp', 'dp'), may hold values from -0.09375 to 0.09375
- gain_first: float32 [1024], replicated, may hold values from 0.1 to 1.9
- shift_first: float32 [1024], replicated, may hold values from -3 to 3
- gain_second: float32 [1024], replicated, may hold values from 0.1 to 1.9
- shift_second: float32 [1024], replicated, may hold values from -3 to 3
Outputs:
- mixed: bfloat16 [14336, 1024], P('dp')
- kv_cache: bfloat16 [14336, 2, 1024], P('dp', None, 'mp')
Inputs may be any that keep to these rules, and one draw needn't show every extreme that they name: page_table is a permutation of the page slots. Page p lies on device p // 14 in arrival order and goes to device page_table[p] // 14; from one device at most 2 pages go to one device, and some pair reaches 2. `segment_ids`: tokens with equal ids form one request; after dealing, a request's tokens are consecutive and lie on one device, which holds at most 4 requests.
All inputs are finite; a program needn't handle non-finite values.
Results may differ from a plain program's by a relative error of at most 0.014.
Values may be sent and summed in bfloat16 or wider, within the bound.
A program may use at most 128 MiB of HBM per device.

v0:
```python
import jax
import jax.numpy as jnp
from jax import lax
from jax.sharding import PartitionSpec as P

HEAD = 64


def layer_norm(hidden_sum, gain, shift):
    center = hidden_sum - jnp.mean(hidden_sum, axis=-1, keepdims=True)
    spread = jnp.mean(center * center, axis=-1, keepdims=True)
    return center * lax.rsqrt(spread + 1e-05) * gain + shift


def attend_head(query, keys, values, segments, block_rows):
    blocks = query.shape[0] // block_rows
    query_blocks = query.reshape(blocks, block_rows, query.shape[1])
    segment_blocks = segments.reshape(blocks, block_rows)

    def per_block(bundle):
        rows, row_ids = bundle
        scores = jnp.einsum("qd,kd->qk", rows, keys, preferred_element_type=jnp.float32) * HEAD ** (
            -0.5
        )
        scores = jnp.where(row_ids[:, None] == segments[None, :], scores, -1e30)
        highest = jnp.max(scores, axis=1, keepdims=True)
        raised = jnp.exp(scores - highest)
        attn_weights = (raised / jnp.sum(raised, axis=1, keepdims=True)).astype(jnp.bfloat16)
        return jnp.dot(attn_weights, values, preferred_element_type=jnp.float32).astype(
            jnp.bfloat16
        )

    return lax.map(per_block, (query_blocks, segment_blocks)).reshape(
        query.shape[0], values.shape[1]
    )


def finish(partial_value, residual, gain, shift):
    total = lax.psum(partial_value.astype(jnp.bfloat16), "mp").astype(jnp.float32)
    return layer_norm(residual.astype(jnp.float32) + total, gain, shift).astype(jnp.bfloat16)


def outgoing_pages(source, got_slots, pages_dev, page):
    paged = source.reshape(pages_dev, page, source.shape[1])[jnp.clip(got_slots, 0, pages_dev - 1)]
    return jnp.where((got_slots >= 0)[:, None, None], paged, jnp.zeros_like(paged))


def body(
    tokens,
    segment_ids,
    page_table,
    w_query,
    w_key,
    w_value,
    w_out,
    w_up,
    w_down,
    gain_first,
    shift_first,
    gain_second,
    shift_second,
):
    n_data = lax.axis_size("dp")
    pages_dev = page_table.shape[0]
    page = tokens.shape[0] // pages_dev
    width = tokens.shape[1]
    slots_per = (pages_dev + n_data - 1) // n_data
    buffer_rows = n_data * slots_per
    target = page_table // pages_dev
    local_slot = page_table % pages_dev
    order = jnp.arange(pages_dev, dtype=jnp.int32)
    earlier = (target[:, None] == target[None, :]) & (order[:, None] < order[None, :])
    rank = jnp.sum(earlier.astype(jnp.int32), axis=0)
    position = target * slots_per + rank
    send_ids = (
        jnp.zeros((buffer_rows, page), jnp.int32)
        .at[position]
        .set(segment_ids.reshape(pages_dev, page))
    )
    send_slots = jnp.full((buffer_rows,), -1, jnp.int32).at[position].set(local_slot)
    send_pages = (
        jnp.zeros((buffer_rows, page, width), tokens.dtype)
        .at[position]
        .set(tokens.reshape(pages_dev, page, width))
    )
    got_pages, got_ids, got_slots = (
        lax.all_to_all(send_pages, "dp", split_axis=0, concat_axis=0, tiled=True),
        lax.all_to_all(send_ids, "dp", split_axis=0, concat_axis=0, tiled=True),
        lax.all_to_all(send_slots, "dp", split_axis=0, concat_axis=0, tiled=True),
    )
    matches = got_slots[None, :] == order[:, None]
    source_row = jnp.sum(
        jnp.where(matches, jnp.arange(buffer_rows, dtype=jnp.int32)[None, :], 0), axis=1
    )
    dealt = got_pages[source_row].reshape(pages_dev * page, got_pages.shape[2])
    dealt_ids = got_ids[source_row].reshape(pages_dev * page)
    full_query, full_key, full_value, full_up, full_out, full_down = (
        lax.all_gather(w_query, "dp", axis=0, tiled=True),
        lax.all_gather(w_key, "dp", axis=0, tiled=True),
        lax.all_gather(w_value, "dp", axis=0, tiled=True),
        lax.all_gather(w_up, "dp", axis=0, tiled=True),
        lax.all_gather(w_out, "dp", axis=1, tiled=True),
        lax.all_gather(w_down, "dp", axis=1, tiled=True),
    )
    query = jnp.dot(dealt, full_query, preferred_element_type=jnp.float32).astype(jnp.bfloat16)
    keys = jnp.dot(dealt, full_key, preferred_element_type=jnp.float32).astype(jnp.bfloat16)
    values = jnp.dot(dealt, full_value, preferred_element_type=jnp.float32).astype(jnp.bfloat16)
    suitable = [
        count for count in range(1, pages_dev + 1) if pages_dev % count == 0 and count * page >= 512
    ]
    block_rows = suitable[0] * page
    heads_here = query.shape[1] // HEAD
    contexts = []
    for head in range(heads_here):
        cols = slice(head * HEAD, (head + 1) * HEAD)
        contexts.append(
            attend_head(query[:, cols], keys[:, cols], values[:, cols], dealt_ids, block_rows)
        )
    context = jnp.concatenate(contexts, axis=1)
    partial_value = jnp.dot(context, full_out, preferred_element_type=jnp.float32)
    first = finish(partial_value, dealt, gain_first, shift_first)
    hidden = jax.nn.gelu(
        jnp.dot(first, full_up, preferred_element_type=jnp.float32), approximate=False
    ).astype(jnp.bfloat16)
    second = finish(
        jnp.dot(hidden, full_down, preferred_element_type=jnp.float32),
        first,
        gain_second,
        shift_second,
    )
    returned = lax.all_to_all(
        outgoing_pages(second, got_slots, pages_dev, page),
        "dp",
        split_axis=0,
        concat_axis=0,
        tiled=True,
    )
    mixed = returned[position].reshape(pages_dev * page, width)
    kv_cache = jnp.stack([keys, values], axis=1)
    return (mixed, kv_cache)


def solution(mesh):
    return jax.shard_map(
        body,
        mesh=mesh,
        in_specs=(
            P("dp", None),
            P("dp"),
            P("dp"),
            P("dp", "mp"),
            P("dp", "mp"),
            P("dp", "mp"),
            P("mp", "dp"),
            P("dp", "mp"),
            P("mp", "dp"),
            P(),
            P(),
            P(),
            P(),
        ),
        out_specs=(P("dp", None), P("dp", None, "mp")),
        check_vma=False,
    )
```

profile of v0, /device:TPU:0, one launch (start us, length us, event | category | flops | bytes accessed | tf_op | source)
XLA Modules:
  0.0 643.9 jit_solution(16866720786995839025)
XLA Ops:
  10.1 7.3 %all-to-all-start = ((s32[8,2,1]{1,2,0:T(1,128)}), s32[8,2,1]{1,2,0:T(1,128)S(1)}, u32[]{:S(2)}, u32[]{:S(2)}) async-start(s32[8,2,1]{1,2,0:T(1,128)} %bitcast.12), calls=%async_computation | async-start | bytes 8192 | tf_op jit(solution)/shard_map/all_to_all | solution.py:89
  18.6 5.2 all-to-all-done
  23.8 3.3 all-to-all-start.2
  27.1 2.5 broadcast.158
  29.6 10.6 %scatter_fusion = bf16[16,128,1024]{2,1,0:T(8,128)(2,1)} fusion(bf16[16,128,1024]{2,1,0:T(8,128)(2,1)} %broadcast.158, s32[14]{0:T(128)S(1)} %compare_select_fusion.2, bf16[14,128,1024]{2,1,0:T(8,128)(2,1)} %bitcast.138), kind=kCustom, calls=%fused_computation.5 | custom fusion | bytes 11010104 | tf_op jit(solution)/shard_map/scatter | solution.py:84
  40.2 6.1 all-to-all-start.1
  46.4 112.6 %all_gather.19 = bf16[1024,256]{1,0:T(8,128)(2,1)S(1)} all-gather(bf16[128,256]{1,0:T(8,128)(2,1)S(1)} %copy-done.14), channel_id=1, replica_groups=mesh['dp'=8,'mp'=4] {'dp'}, dimensions={0}, use_global_device_ids=true | all-gather | bytes 589824 | tf_op jit(solution)/shard_map/all_gather | solution.py:99
  159.0 31.5 %all_gather.20 = bf16[1024,256]{1,0:T(8,128)(2,1)S(1)} all-gather(bf16[128,256]{1,0:T(8,128)(2,1)S(1)} %copy-done.15), channel_id=1, replica_groups=mesh['dp'=8,'mp'=4] {'dp'}, dimensions={0}, use_global_device_ids=true | all-gather | bytes 589824 | tf_op jit(solution)/shard_map/all_gather | solution.py:100
  190.5 31.4 %all_gather.18 = bf16[1024,256]{1,0:T(8,128)(2,1)S(1)} all-gather(bf16[128,256]{1,0:T(8,128)(2,1)S(1)} %copy-done.16), channel_id=1, replica_groups=mesh['dp'=8,'mp'=4] {'dp'}, dimensions={0}, use_global_device_ids=true | all-gather | bytes 589824 | tf_op jit(solution)/shard_map/all_gather | solution.py:98
  221.9 28.4 %all_gather.21 = bf16[256,1024]{1,0:T(8,128)(2,1)} all-gather(bf16[256,128]{1,0:T(8,128)(2,1)S(1)} %copy-done.17), channel_id=1, replica_groups=mesh['dp'=8,'mp'=4] {'dp'}, dimensions={1}, use_global_device_ids=true | all-gather | bytes 589824 | tf_op jit(solution)/shard_map/all_gather | solution.py:102
  250.9 1.3 clamp_reduce_fusion
  252.9 4.9 gather_fusion
  257.8 3.2 convolution_convert_fusion.3
  262.9 3.2 convolution_convert_fusion.2
  268.1 3.2 convolution_convert_fusion.4
  272.4 7.8 %while.40 = (s32[]{:T(128)}, bf16[2,896,64]{1,2,0:T(8,128)(2,1)S(1)}, s32[2,896]{1,0:T(2,128)S(1)}, s32[14,128]{1,0:T(8,128)S(1)}, bf16[2,896,64]{2,1,0:T(8,128)...) while((s32[]{:T(128)}, bf16[2,896,64]{1,2,0:T(8,128)(2,1)S(1)}, ...), condition=%wide.region_8.9_spmd, body=%wide.region_5.8_spmd.sunk | while | flops 425548032 | bytes 20567648 | solution.py:33
  274.9 1.5 fusion.144
  278.7 1.5 fusion.144
  281.8 7.7 %while.41 = (s32[]{:T(128)}, bf16[2,896,64]{1,2,0:T(8,128)(2,1)S(1)}, s32[2,896]{1,0:T(2,128)S(1)}, s32[14,128]{1,0:T(8,128)S(1)}, bf16[2,896,64]{2,1,0:T(8,128)...) while((s32[]{:T(128)}, bf16[2,896,64]{1,2,0:T(8,128)(2,1)S(1)}, ...), condition=%wide.region_12.13_spmd, body=%wide.region_9.12_spmd.sunk | while | flops 425548032 | bytes 20567648 | solution.py:33
  284.1 1.5 fusion.149
  285.7 1.2 fusion.147
  287.9 1.5 fusion.149
  290.4 7.7 %while.42 = (s32[]{:T(128)}, bf16[2,896,64]{1,2,0:T(8,128)(2,1)S(1)}, s32[2,896]{1,0:T(2,128)S(1)}, s32[14,128]{1,0:T(8,128)S(1)}, bf16[2,896,64]{2,1,0:T(8,128)...) while((s32[]{:T(128)}, bf16[2,896,64]{1,2,0:T(8,128)(2,1)S(1)}, ...), condition=%wide.region_16.17_spmd, body=%wide.region_13.16_spmd.sunk | while | flops 425548032 | bytes 20567648 | solution.py:33
  290.4 1.2 fusion.152
  292.7 1.5 fusion.154
  294.3 1.2 fusion.152
  296.5 1.5 fusion.154
  299.0 7.9 %while.43 = (s32[]{:T(128)}, bf16[2,896,64]{1,2,0:T(8,128)(2,1)S(1)}, s32[2,896]{1,0:T(2,128)S(1)}, s32[14,128]{1,0:T(8,128)S(1)}, bf16[2,896,64]{2,1,0:T(8,128)...) while((s32[]{:T(128)}, bf16[2,896,64]{1,2,0:T(8,128)(2,1)S(1)}, ...), condition=%wide.region_20.21_spmd, body=%wide.region_17.20_spmd.sunk | while | flops 425548032 | bytes 20567648 | solution.py:33
  301.5 1.5 fusion.159
  305.3 1.5 fusion.159
  306.9 3.0 convolution_convert_fusion
  311.2 73.7 %all-reduce.3.cloned.1.call-done = bf16[1792,1024]{1,0:T(8,128)(2,1)} async-done(((bf16[1792,1024]{1,0:T(8,128)(2,1)}), bf16[1792,1024]{1,0:T(8,128)(2,1)}) %all-reduce.3.cloned.1.call-update) | async-done | bytes 3670032 | tf_op jit(solution)/shard_map/psum | solution.py:39
  384.9 4.3 fusion.43
  390.5 2.3 multiply_reduce_fusion.1
  392.8 3.3 add_convert_fusion.1
  396.1 14.5 %all-gather.5.cloned.1.call-done = bf16[1024,1024]{1,0:T(8,128)(2,1)} async-done(((bf16[1024,128]{1,0:T(8,128)(2,1)}), bf16[1024,1024]{1,0:T(8,128)(2,1)}) %all-gather.5.cloned.1.call-update) | async-done | bytes 2097168 | tf_op jit(solution)/shard_map/all_gather | solution.py:103
  410.5 25.9 %convolution_convert_fusion.1 = bf16[1792,1024]{1,0:T(8,128)(2,1)} fusion(bf16[1024,1024]{1,0:T(8,128)(2,1)} %all-gather.5.cloned.1.call-done, bf16[1792,1024]{1,0:T(8,128)(2,1)} %add_convert_fusion.1, bf16[1024,1024]{1,0:T(8,128)(2,1)} %all-gather.3.cloned.1.call-done), kind=kOutput, calls=%fused_computation.86 | convolution fusion | flops 7637303296 | bytes 11534336 | tf_op jit(solution)/shard_map/dot_general | solution.py:126
  436.6 75.1 %all-reduce.5.cloned.1.call-done = bf16[1792,1024]{1,0:T(8,128)(2,1)} async-done(((bf16[1792,1024]{1,0:T(8,128)(2,1)}), bf16[1792,1024]{1,0:T(8,128)(2,1)}) %all-reduce.5.cloned.1.call-update) | async-done | bytes 3670032 | tf_op jit(solution)/shard_map/psum | solution.py:39
  511.8 4.3 fusion.45
  517.1 2.6 multiply_reduce_fusion
  519.7 3.3 add_convert_fusion
  523.0 4.8 gather_fusion.2
  527.8 4.6 broadcast_select_fusion
  532.4 5.5 all-to-all-start.3
  538.0 1.4 pad_maximum_fusion
  539.3 3.6 copy.80
  542.9 88.2 %all-to-all-done.3 = bf16[16,128,1024]{2,1,0:T(8,128)(2,1)} async-done(((bf16[16,128,1024]{2,1,0:T(8,128)(2,1)}), bf16[16,128,1024]{2,1,0:T(8,128)(2,1)}, u32[]{:S(2)}, u32[]{:S(2)}) %all-to-all-start.3) | async-done | bytes 4194336 | tf_op jit(solution)/shard_map/all_to_all | solution.py:131
  631.1 4.9 gather_fusion.3
  (131 shorter events, 30.9 us)
Async XLA Ops:
  8.0 9.4 %copy-start = (s32[1792]{0:T(1024)S(1)}, s32[1792]{0:T(1024)}, u32[]{:S(2)}) copy-start(s32[1792]{0:T(1024)} %param.22) | copy-start | bytes 21508
  8.8 31.4 %copy-start.23 = (s32[14]{0:T(128)}, s32[14]{0:T(128)S(1)}, u32[]{:S(2)}) copy-start(s32[14]{0:T(128)S(1)} %compare_select_fusion.2) | copy-start | bytes 172
  10.1 13.7 %all-to-all-start = ((s32[8,2,1]{1,2,0:T(1,128)}), s32[8,2,1]{1,2,0:T(1,128)S(1)}, u32[]{:S(2)}, u32[]{:S(2)}) async-start(s32[8,2,1]{1,2,0:T(1,128)} %bitcast.12), calls=%async_computation | async-start | bytes 8192 | tf_op jit(solution)/shard_map/all_to_all | solution.py:89
  23.8 16.5 %all-to-all-start.2 = ((s32[8,2,128]{2,1,0:T(2,128)}), s32[8,2,128]{2,1,0:T(2,128)S(1)}, u32[]{:S(2)}, u32[]{:S(2)}) async-start(s32[8,2,128]{2,1,0:T(2,128)} %bitcast.18), calls=%async_computation.2 | async-start | bytes 16384 | tf_op jit(solution)/shard_map/all_to_all | solution.py:88
  40.2 6.2 copy-start.14
  40.2 118.8 %copy-start.15 = (bf16[128,256]{1,0:T(8,128)(2,1)S(1)}, bf16[128,256]{1,0:T(8,128)(2,1)}, u32[]{:S(2)}) copy-start(bf16[128,256]{1,0:T(8,128)(2,1)} %param.26) | copy-start | bytes 196612
  40.2 150.3 %copy-start.16 = (bf16[128,256]{1,0:T(8,128)(2,1)S(1)}, bf16[128,256]{1,0:T(8,128)(2,1)}, u32[]{:S(2)}) copy-start(bf16[128,256]{1,0:T(8,128)(2,1)} %param.24) | copy-start | bytes 196612
  40.2 181.7 %copy-start.17 = (bf16[256,128]{1,0:T(8,128)(2,1)S(1)}, bf16[256,128]{1,0:T(8,128)(2,1)}, u32[]{:S(2)}) copy-start(bf16[256,128]{1,0:T(8,128)(2,1)} %param.27) | copy-start | bytes 196612
  40.2 212.7 %all-to-all-start.1 = ((bf16[16,128,1024]{2,1,0:T(8,128)(2,1)}), bf16[16,128,1024]{2,1,0:T(8,128)(2,1)}, u32[]{:S(2)}, u32[]{:S(2)}) async-start(bf16[16,128,1024]{2,1,0:T(8,128)(2,1)} %scatter_fusion), calls=%async_computation.1 | async-start | bytes 8388608 | tf_op jit(solution)/shard_map/all_to_all | solution.py:87
  46.3 338.6 %all-reduce.3.cloned.1.call-start = ((), (), s32[]{:S(2)}) async-start(), calls=%async_computation.4 | async-start | bytes 7340032 | tf_op jit(solution)/shard_map/psum | solution.py:39
  252.2 8.8 %copy-start.25 = (s32[16]{0:T(128)}, s32[16]{0:T(128)S(1)}, u32[]{:S(2)}) copy-start(s32[16]{0:T(128)S(1)} %all_to_all.24) | copy-start | bytes 196
  261.0 0.9 copy-start.6
  266.2 0.9 copy-start.8
  290.4 7.7 %copy-start.9 = (bf16[1792,64]{0,1:T(8,128)(2,1)S(1)}, bf16[1792,64]{0,1:T(8,128)(2,1)}, u32[]{:S(2)}) copy-start(bf16[1792,64]{0,1:T(8,128)(2,1)} %get-tuple-element.345) | copy-start | bytes 688132
  290.4 8.0 %copy-start.10 = (bf16[1792,64]{0,1:T(8,128)(2,1)S(1)}, bf16[1792,64]{0,1:T(8,128)(2,1)}, u32[]{:S(2)}) copy-start(bf16[1792,64]{0,1:T(8,128)(2,1)} %get-tuple-element.341) | copy-start | bytes 688132
  290.4 8.3 %copy-start.11 = (bf16[1792,64]{0,1:T(8,128)(2,1)S(1)}, bf16[1792,64]{0,1:T(8,128)(2,1)}, u32[]{:S(2)}) copy-start(bf16[1792,64]{0,1:T(8,128)(2,1)} %get-tuple-element.349) | copy-start | bytes 688132
  299.0 7.9 %copy-start.12 = (bf16[256,1024]{1,0:T(8,128)(2,1)S(1)}, bf16[256,1024]{1,0:T(8,128)(2,1)}, u32[]{:S(2)}) copy-start(bf16[256,1024]{1,0:T(8,128)(2,1)} %all_gather.21) | copy-start | bytes 1572868
  299.0 7.9 %copy-start.13 = (bf16[2,8,8,896]{3,2,0,1:T(8,128)(2,1)S(1)}, bf16[2,8,8,896]{3,2,0,1:T(8,128)(2,1)}, u32[]{:S(2)}) copy-start(bf16[2,8,8,896]{3,2,0,1:T(8,128)(2,1)} %copy.85) | copy-start | bytes 688132
  309.9 86.2 %all-gather.3.cloned.1.call-start = ((), (), s32[]{:S(2)}) async-start(), calls=%async_computation.5 | async-start | bytes 2359296 | tf_op jit(solution)/shard_map/all_gather | solution.py:101
  310.5 100.0 %all-gather.5.cloned.1.call-start = ((), (), s32[]{:S(2)}) async-start(), calls=%async_computation.6 | async-start | bytes 2359296 | tf_op jit(solution)/shard_map/all_gather | solution.py:103
  311.1 81.6 %copy-start.19 = (f32[1024]{0:T(1024)S(1)}, f32[1024]{0:T(1024)}, u32[]{:S(2)}) copy-start(f32[1024]{0:T(1024)} %param.31) | copy-start | bytes 12292
  311.1 81.6 %copy-start.20 = (f32[1024]{0:T(1024)S(1)}, f32[1024]{0:T(1024)}, u32[]{:S(2)}) copy-start(f32[1024]{0:T(1024)} %param.30) | copy-start | bytes 12292
  311.1 200.6 %all-reduce.5.cloned.1.call-start = ((), (), s32[]{:S(2)}) async-start(), calls=%async_computation.7 | async-start | bytes 7340032 | tf_op jit(solution)/shard_map/psum | solution.py:39
  384.9 4.3 copy-start.2
  384.9 5.5 copy-start.4
  396.1 40.4 %copy-start.18 = (s32[8,2]{1,0:T(8,128)S(1)}, s32[8,2]{1,0:T(8,128)}, u32[]{:S(2)}) copy-start(s32[8,2]{1,0:T(8,128)} %get-tuple-element.274) | copy-start | bytes 196
  396.1 40.5 %copy-start.26 = (s32[16]{0:T(128)S(1)}, s32[16]{0:T(128)}, u32[]{:S(2)}) copy-start(s32[16]{0:T(128)} %copy-done.25) | copy-start | bytes 196
  436.6 83.1 %copy-start.21 = (f32[1024]{0:T(1024)S(1)}, f32[1024]{0:T(1024)}, u32[]{:S(2)}) copy-start(f32[1024]{0:T(1024)} %param.33) | copy-start | bytes 12292
  436.6 83.1 %copy-start.22 = (f32[1024]{0:T(1024)S(1)}, f32[1024]{0:T(1024)}, u32[]{:S(2)}) copy-start(f32[1024]{0:T(1024)} %param.32) | copy-start | bytes 12292
  511.8 4.3 copy-start.3
  511.8 5.3 copy-start.5
  527.8 10.1 %copy-start.24 = (s32[14]{0:T(128)S(1)}, s32[14]{0:T(128)}, u32[]{:S(2)}) copy-start(s32[14]{0:T(128)} %copy-done.23) | copy-start | bytes 172
  527.8 10.1 %copy-start.7 = (bf16[1792,256]{0,1:T(8,128)(2,1)S(1)}, bf16[1792,256]{0,1:T(8,128)(2,1)}, u32[]{:S(2)}) copy-start(bf16[1792,256]{0,1:T(8,128)(2,1)} %copy-done.6) | copy-start | bytes 2752516
  532.4 98.7 %all-to-all-start.3 = ((bf16[16,128,1024]{2,1,0:T(8,128)(2,1)}), bf16[16,128,1024]{2,1,0:T(8,128)(2,1)}, u32[]{:S(2)}, u32[]{:S(2)}) async-start(bf16[16,128,1024]{2,1,0:T(8,128)(2,1)} %broadcast_select_fusion), calls=%async_computation.3 | async-start | bytes 8388608 | tf_op jit(solution)/shard_map/all_to_all | solution.py:131
  537.9 98.0 %copy-start.1 = (s32[1792]{0:T(1024)S(1)}, s32[1792]{0:T(1024)}, u32[]{:S(2)}) copy-start(s32[1792]{0:T(1024)} %param.22) | copy-start | bytes 21508
Sparse Core Ops, SparseCore 0:
  310.1 74.8 all-reduce.2
  436.6 75.1 all-reduce.4
Sparse Core Ops, SparseCore 1:
  312.5 47.1 all-gather.2
  361.6 48.8 all-gather.4
where the time goes:
time: 650 us; the launch traced here: 644 us
  waiting for transfers between devices  258 us (40%)
  blocking collectives  204 us (31%)
  matrix products  60.6 us (9%)
  local copies, waits for them, and re-layouts  45.5 us (7%)
  other arithmetic  36.5 us (6%)
  starting transfers between devices  22.4 us (3%)
  between operations  16.5 us (3%)
    psum x2, waiting for transfers between devices, finish(): lax.psum(partial_value.astype(jnp.bfloat16), 'mp').astype(jnp.float32)  149 us
    all_gather x1, blocking collectives, body(): lax.all_gather(w_key, 'dp', axis=0, tiled=True)  113 us
    all_to_all x1, waiting for transfers between devices, body(): lax.all_to_all(outgoing_pages(second, got_slots, pages_dev, page), 'dp',...  88.2 us
    all_gather x1, blocking collectives, body(): lax.all_gather(w_value, 'dp', axis=0, tiled=True)  31.5 us
    all_gather x1, blocking collectives, body(): lax.all_gather(w_query, 'dp', axis=0, tiled=True)  31.4 us
    all_gather x1, blocking collectives, body(): lax.all_gather(w_out, 'dp', axis=1, tiled=True)  28.4 us
    dot_general x1, matrix products, body(): jnp.dot(hidden, full_down, preferred_element_type=jnp.float32)  25.9 us
    all_gather x1, waiting for transfers between devices, body(): lax.all_gather(w_down, 'dp', axis=1, tiled=True)  14.5 us
  transfers between devices with their start and end apart: 8, of which 5 were waited for; matrix products, arithmetic and copies ran while one was open for 5% of the time, Pallas kernels for 0%

commit v1 on v0

v1 whole, which is shorter than its diff:
```python
import functools

import jax
import jax.numpy as jnp
from jax import lax
from jax.experimental import pallas as pl
from jax.experimental.pallas import tpu as pltpu
from jax.sharding import PartitionSpec as P

HEAD = 64
MESH = pl.DeviceIdType.MESH
VMEM_BYTES = 48 * 1024 * 1024


def mp_peers(me_m, n_mp):
    return me_m + 1 - 2 * lax.rem(me_m, 2), lax.rem(me_m + 2, n_mp)


def swap_kernel(n_dp, n_mp, with_extra, *refs):
    if with_extra:
        send, meta, weight, recv, got_meta, full, *sems = refs
    else:
        send, recv, *sems = refs
    local, a_send, a_recv, f_send, f_recv, *more = sems
    me_d, me_m = lax.axis_index("dp"), lax.axis_index("mp")
    sib, far = mp_peers(me_m, n_mp)
    barrier = pltpu.get_barrier_semaphore()
    for k in range(1, n_dp):
        pl.semaphore_signal(
            barrier, inc=1, device_id=(lax.rem(me_d + k, n_dp), me_m), device_id_type=MESH
        )
    for peer in (sib, far):
        pl.semaphore_signal(barrier, inc=1, device_id=(me_d, peer), device_id_type=MESH)
    pl.semaphore_wait(barrier, n_dp + 1)

    def remote(src, dst, s_sem, r_sem, dev):
        return pltpu.make_async_remote_copy(
            src_ref=src,
            dst_ref=dst,
            send_sem=s_sem,
            recv_sem=r_sem,
            device_id=dev,
            device_id_type=MESH,
        )

    def source(k):
        return lax.rem(me_d - k + n_dp, n_dp)

    own = pltpu.make_async_copy(send.at[me_d], recv.at[me_d, :, me_m], local.at[0])
    own.start()
    outs = []
    if with_extra:
        m_send, m_recv, z_send, z_recv, y_send, y_recv = more
        own_meta = pltpu.make_async_copy(meta.at[me_d], got_meta.at[me_d], local.at[1])
        own_meta.start()
        own_w = pltpu.make_async_copy(weight, full.at[me_d], local.at[2])
        own_w.start()
        for k in range(1, n_dp):
            to = lax.rem(me_d + k, n_dp)
            outs.append(
                remote(meta.at[to], got_meta.at[me_d], m_send.at[k], m_recv.at[k], (to, me_m))
            )
            outs[-1].start()
    for k in range(1, n_dp):
        to = lax.rem(me_d + k, n_dp)
        outs.append(
            remote(send.at[to], recv.at[me_d, :, me_m], a_send.at[k], a_recv.at[k], (to, me_m))
        )
        outs[-1].start()
    if with_extra:
        rows = n_dp // 2
        b = lax.rem(me_d, 2)
        a = (me_d - b) // 2
        across = me_d + 1 - 2 * b
        outs.append(remote(weight, full.at[me_d], y_send.at[0], y_recv.at[0], (me_d + 1 - 2 * b, me_m)))
        outs[-1].start()
        for k in range(1, rows):
            to = lax.rem(a + k, rows) * 2 + b
            outs.append(remote(weight, full.at[me_d], z_send.at[k], z_recv.at[k], (to, me_m)))
            outs[-1].start()

    def hand_on(k):
        block = recv.at[source(k), :, me_m]
        for way, peer in ((0, far), (1, sib)):
            outs.append(
                remote(block, block, f_send.at[way, k], f_recv.at[way, k], (me_d, peer))
            )
            outs[-1].start()

    def hand_far(k):
        block = recv.at[source(k), :, far]
        remote(block, block, f_send.at[0, k], f_recv.at[0, k], (me_d, far)).wait_recv()
        outs.append(remote(block, block, f_send.at[2, k], f_recv.at[2, k], (me_d, sib)))
        outs[-1].start()

    own.wait()
    hand_on(0)
    for k in range(1, n_dp):
        block = recv.at[source(k), :, me_m]
        remote(block, block, a_send.at[k], a_recv.at[k], (me_d, far)).wait_recv()
        hand_on(k)
        hand_far(k - 1)
    hand_far(n_dp - 1)
    if with_extra:
        for k in range(1, rows):
            block = full.at[lax.rem(a - k + rows, rows) * 2 + b]
            remote(block, block, z_send.at[k], z_recv.at[k], (across, me_m)).wait_recv()
            outs.append(remote(block, block, y_send.at[k], y_recv.at[k], (across, me_m)))
            outs[-1].start()
        for k in range(rows):
            block = full.at[lax.rem(a - k + rows, rows) * 2 + 1 - b]
            remote(block, block, y_send.at[k], y_recv.at[k], (across, me_m)).wait_recv()
        for k in range(1, n_dp):
            block = got_meta.at[source(k)]
            remote(block, block, m_send.at[k], m_recv.at[k], (across, me_m)).wait_recv()
        own_meta.wait()
        own_w.wait()
    sib_far = lax.rem(sib + 2, n_mp)
    for k in range(n_dp):
        for way, quarter in ((1, sib), (2, sib_far)):
            block = recv.at[source(k), :, quarter]
            remote(block, block, f_send.at[way, k], f_recv.at[way, k], (me_d, sib)).wait_recv()
    for copy in outs:
        copy.wait_send()


def swap(send, n_mp, collective_id, meta=None, weight=None):
    n_dp, slots, rows, width = send.shape
    with_extra = meta is not None
    any_spec = pl.BlockSpec(memory_space=pl.ANY)
    outs = [jax.ShapeDtypeStruct((n_dp, slots, n_mp, rows, width), send.dtype)]
    sems = [(3,), (n_dp,), (n_dp,), (3, n_dp), (3, n_dp)]
    args = [send]
    if with_extra:
        outs += [
            jax.ShapeDtypeStruct(meta.shape, meta.dtype),
            jax.ShapeDtypeStruct((n_dp, *weight.shape), weight.dtype),
        ]
        sems += [(n_dp,), (n_dp,)] + [(n_dp // 2,)] * 4
        args += [meta, weight]
    return pl.pallas_call(
        functools.partial(swap_kernel, n_dp, n_mp, with_extra),
        out_shape=outs,
        in_specs=[any_spec] * len(args),
        out_specs=[any_spec] * len(outs),
        scratch_shapes=[pltpu.SemaphoreType.DMA(s) for s in sems],
        compiler_params=pltpu.CompilerParams(collective_id=collective_id, has_side_effects=True),
        name=f"swap_{collective_id}",
    )(*args)


def reduce_kernel(n_mp, chunk, gather, *refs):
    part, resid, gain, shift, out, sib_in, acc, far_in, res, *sems = refs
    local, s_send, s_recv, x_send, x_recv, *more = sems
    me_d, me_m = lax.axis_index("dp"), lax.axis_index("mp")
    sib, far = mp_peers(me_m, n_mp)
    sib_far = lax.rem(sib + 2, n_mp)
    chunks = part.shape[0] // chunk
    barrier = pltpu.get_barrier_semaphore()
    for peer in (sib, far):
        pl.semaphore_signal(barrier, inc=1, device_id=(me_d, peer), device_id_type=MESH)
    pl.semaphore_wait(barrier, 2)
    if gather:
        own = pltpu.make_async_copy(resid.at[:, me_m], res, local.at[0])
    else:
        own = pltpu.make_async_copy(resid.at[:, me_m], res, local.at[0])
    own.start()

    def at(c):
        return pl.ds(c * chunk, chunk)

    def to_sib(half, c):
        quarter = sib_far if half == 0 else sib
        return pltpu.make_async_remote_copy(
            src_ref=part.at[at(c), quarter],
            dst_ref=sib_in.at[half, at(c)],
            send_sem=s_send.at[half, c],
            recv_sem=s_recv.at[half, c],
            device_id=(me_d, sib),
            device_id_type=MESH,
        )

    def to_far(c):
        return pltpu.make_async_remote_copy(
            src_ref=acc.at[at(c)],
            dst_ref=far_in.at[at(c)],
            send_sem=x_send.at[c],
            recv_sem=x_recv.at[c],
            device_id=(me_d, far),
            device_id_type=MESH,
        )

    def spread(way, c, quarter):
        g_send, g_recv = more
        block = out.at[at(c), quarter]
        return pltpu.make_async_remote_copy(
            src_ref=block,
            dst_ref=block,
            send_sem=g_send.at[way, c],
            recv_sem=g_recv.at[way, c],
            device_id=(me_d, far if way == 0 else sib),
            device_id_type=MESH,
        )

    for half in (0, 1):
        for c in range(chunks):
            to_sib(half, c).start()

    def add_far(c, _):
        to_sib(0, c).wait_recv()
        mine = part[at(c), far].astype(jnp.float32) + sib_in[0, at(c)].astype(jnp.float32)
        acc[at(c)] = mine.astype(acc.dtype)
        to_far(c).start()
        return 0

    lax.fori_loop(0, chunks, add_far, 0)
    own.wait()

    def settle(c, _):
        to_sib(1, c).wait_recv()
        to_far(c).wait_recv()
        total = (
            part[at(c), me_m].astype(jnp.float32)
            + sib_in[1, at(c)].astype(jnp.float32)
            + far_in[at(c)].astype(jnp.float32)
            + res[at(c)].astype(jnp.float32)
        )
        center = total - jnp.mean(total, axis=-1, keepdims=True)
        spread_sq = jnp.mean(center * center, axis=-1, keepdims=True)
        normed = center * lax.rsqrt(spread_sq + 1e-05) * gain[...] + shift[...]
        if gather:
            out[at(c), me_m] = normed.astype(out.dtype)
            spread(0, c, me_m).start()
            spread(1, c, me_m).start()
        else:
            out[at(c)] = normed.astype(out.dtype)
        return 0

    lax.fori_loop(0, chunks, settle, 0)
    if gather:

        def pass_on(c, _):
            spread(0, c, far).wait_recv()
            spread(2, c, far).start()
            return 0

        lax.fori_loop(0, chunks, pass_on, 0)
        for c in range(chunks):
            spread(1, c, sib).wait_recv()
            spread(2, c, sib_far).wait_recv()
            for way, quarter in ((0, me_m), (1, me_m), (2, far)):
                spread(way, c, quarter).wait_send()
    for c in range(chunks):
        to_sib(0, c).wait_send()
        to_sib(1, c).wait_send()
        to_far(c).wait_send()


def reduce_norm(part, resid, gain, shift, gather, collective_id):
    pages, n_mp, rows, width = part.shape
    chunk = 2 if pages % 2 == 0 else 1
    chunks = pages // chunk
    quarter = (pages, rows, width)
    vmem = pl.BlockSpec(memory_space=pltpu.VMEM)
    sems = [(1,), (2, chunks), (2, chunks), (chunks,), (chunks,)]
    if gather:
        sems += [(3, chunks), (3, chunks)]
    return pl.pallas_call(
        functools.partial(reduce_kernel, n_mp, chunk, gather),
        out_shape=jax.ShapeDtypeStruct(part.shape if gather else quarter, part.dtype),
        in_specs=[vmem, pl.BlockSpec(memory_space=pl.ANY), vmem, vmem],
        out_specs=vmem,
        scratch_shapes=[
            pltpu.VMEM((2, *quarter), part.dtype),
            pltpu.VMEM(quarter, part.dtype),
            pltpu.VMEM(quarter, part.dtype),
            pltpu.VMEM(quarter, part.dtype),
        ]
        + [pltpu.SemaphoreType.DMA(s) for s in sems],
        compiler_params=pltpu.CompilerParams(
            collective_id=collective_id, has_side_effects=True, vmem_limit_bytes=VMEM_BYTES
        ),
        name=f"reduce_{collective_id}",
    )(part, resid, gain.reshape(1, 1, width), shift.reshape(1, 1, width))


def pick_kernel(rows_ref, src, out):
    out[...] = src[...]


def pick(table, source, part=None):
    count = table.shape[0]
    if part is None:
        block = (1, *source.shape[1:])
        tail = (0,) * (source.ndim - 1)
        index = lambda i, t: (t[i], *tail)
        out_block, out_index = block, lambda i, t: (i, *tail)
        scalars = table
    else:
        block = (1, 1, *source.shape[2:])
        index = lambda i, t: (t[i], t[count], 0, 0)
        out_block, out_index = block, lambda i, t: (i, 0, 0, 0)
        scalars = jnp.concatenate([table, part.reshape(1)])
    return pl.pallas_call(
        pick_kernel,
        out_shape=jax.ShapeDtypeStruct((count, *out_block[1:]), source.dtype),
        grid_spec=pltpu.PrefetchScalarGridSpec(
            num_scalar_prefetch=1,
            grid=(count,),
            in_specs=[pl.BlockSpec(block, index)],
            out_specs=pl.BlockSpec(out_block, out_index),
        ),
        name="pick",
    )(scalars, source)


def project_kernel(rows_ref, src, weight, dealt, query, keys, values):
    page = src[0]
    dealt[0] = page
    width = query.shape[1]
    both = jnp.dot(page, weight[:, : 3 * width], preferred_element_type=jnp.float32)
    query[...] = both[:, :width].astype(query.dtype)
    keys[...] = both[:, width : 2 * width].astype(keys.dtype)
    values[...] = both[:, 2 * width :].astype(values.dtype)


def project(source_row, got, weight):
    count = source_row.shape[0]
    _, page, width = got.shape
    cols = weight.shape[1] // 4
    flat = jax.ShapeDtypeStruct((count * page, cols), got.dtype)
    flat_spec = pl.BlockSpec((page, cols), lambda i, t: (i, 0))
    return pl.pallas_call(
        project_kernel,
        out_shape=[jax.ShapeDtypeStruct((count, page, width), got.dtype), flat, flat, flat],
        grid_spec=pltpu.PrefetchScalarGridSpec(
            num_scalar_prefetch=1,
            grid=(count,),
            in_specs=[
                pl.BlockSpec((1, page, width), lambda i, t: (t[i], 0, 0)),
                pl.BlockSpec(weight.shape, lambda i, t: (0, 0)),
            ],
            out_specs=[
                pl.BlockSpec((1, page, width), lambda i, t: (i, 0, 0)),
                flat_spec,
                flat_spec,
                flat_spec,
            ],
        ),
        compiler_params=pltpu.CompilerParams(vmem_limit_bytes=VMEM_BYTES),
        name="project",
    )(source_row, got, weight)


def attend_kernel(query, keys, values, row_ids, col_ids, weight, out):
    width = query.shape[1]
    lane = lax.broadcasted_iota(jnp.int32, (1, width), 1)
    same = row_ids[...] == col_ids[...]
    rows = query[...].astype(jnp.float32) * HEAD**-0.5
    context = jnp.zeros(query.shape, jnp.float32)
    for head in range(width // HEAD):
        here = (lane >= head * HEAD) & (lane < (head + 1) * HEAD)
        picked = jnp.where(here, rows, 0.0).astype(query.dtype)
        scores = lax.dot_general(
            picked, keys[...], (((1,), (1,)), ((), ())), preferred_element_type=jnp.float32
        )
        scores = jnp.where(same, scores, -1e30)
        raised = jnp.exp(scores - jnp.max(scores, axis=1, keepdims=True))
        total = jnp.sum(raised, axis=1, keepdims=True)
        mixed = jnp.dot(
            raised.astype(values.dtype), values[...], preferred_element_type=jnp.float32
        )
        context = jnp.where(here, mixed / total, context)
    out[...] = lax.dot_general(
        context.astype(query.dtype),
        weight[...],
        (((1,), (1,)), ((), ())),
        preferred_element_type=jnp.float32,
    ).astype(out.dtype)


def attend(query, keys, values, ids, weight):
    tokens, width = query.shape
    block = 256 if tokens % 256 == 0 else 128
    whole = pl.BlockSpec((tokens, width), lambda i: (0, 0))
    features = weight.shape[0]
    return pl.pallas_call(
        attend_kernel,
        out_shape=jax.ShapeDtypeStruct((tokens, features), query.dtype),
        grid=(tokens // block,),
        in_specs=[
            pl.BlockSpec((block, width), lambda i: (i, 0)),
            whole,
            whole,
            pl.BlockSpec((block, 1), lambda i: (i, 0)),
            pl.BlockSpec((1, tokens), lambda i: (0, 0)),
            pl.BlockSpec((features, width), lambda i: (0, 3)),
        ],
        out_specs=pl.BlockSpec((block, features), lambda i: (i, 0)),
        compiler_params=pltpu.CompilerParams(vmem_limit_bytes=VMEM_BYTES),
        name="attend",
    )(query, keys, values, ids.reshape(tokens, 1), ids.reshape(1, tokens), weight)


def body(
    tokens,
    segment_ids,
    page_table,
    w_query,
    w_key,
    w_value,
    w_out,
    w_up,
    w_down,
    gain_first,
    shift_first,
    gain_second,
    shift_second,
):
    n_data, n_mp = lax.axis_size("dp"), lax.axis_size("mp")
    me_m = lax.axis_index("mp").astype(jnp.int32)
    pages_dev = page_table.shape[0]
    page = tokens.shape[0] // pages_dev
    width = tokens.shape[1]
    rows = page // n_mp
    slots_per = (pages_dev + n_data - 1) // n_data
    buffer_rows = n_data * slots_per
    target = page_table // pages_dev
    local_slot = page_table % pages_dev
    order = jnp.arange(pages_dev, dtype=jnp.int32)
    earlier = (target[:, None] == target[None, :]) & (order[:, None] < order[None, :])
    rank = jnp.sum(earlier.astype(jnp.int32), axis=0)
    position = target * slots_per + rank
    places = jnp.arange(buffer_rows, dtype=jnp.int32)
    placed = position[None, :] == places[:, None]
    page_of = jnp.sum(jnp.where(placed, order[None, :], 0), axis=1)
    ids_paged = segment_ids.reshape(pages_dev, page)
    send_ids = jnp.sum(jnp.where(placed[:, :, None], ids_paged[None], 0), axis=1)
    send_slots = jnp.sum(jnp.where(placed, local_slot[None, :] + 1, 0), axis=1) - 1
    meta = jnp.concatenate(
        [
            send_ids[:, None, :],
            jnp.broadcast_to(send_slots[:, None, None], (buffer_rows, 7, page)),
        ],
        axis=1,
    ).reshape(n_data, slots_per, 8, page)
    weight = jnp.concatenate([w_query, w_key, w_value, w_out.T], axis=1)
    send = pick(page_of, tokens.reshape(pages_dev, n_mp, rows, width), me_m)
    got, got_meta, full = swap(
        send.reshape(n_data, slots_per, rows, width), n_mp, 1, meta, weight
    )
    full_up = lax.all_gather(w_up, "dp", axis=0, tiled=True)
    full_down = lax.all_gather(w_down, "dp", axis=1, tiled=True)
    full = full.reshape(width, weight.shape[1])
    got_meta = got_meta.reshape(buffer_rows, 8, page)
    got_slots = got_meta[:, 1, 0]
    matches = got_slots[None, :] == order[:, None]
    source_row = jnp.sum(jnp.where(matches, places[None, :], 0), axis=1)
    dealt_ids = jnp.sum(jnp.where(matches[:, :, None], got_meta[None, :, 0, :], 0), axis=1)
    dealt, query, keys, values = project(source_row, got.reshape(buffer_rows, page, width), full)
    term = attend(query, keys, values, dealt_ids.reshape(-1), full)
    split = (pages_dev, n_mp, rows, width)
    first = reduce_norm(term.reshape(split), dealt.reshape(split), gain_first, shift_first, True, 2)
    hidden = jax.nn.gelu(
        jnp.dot(
            first.reshape(pages_dev * page, width), full_up, preferred_element_type=jnp.float32
        ),
        approximate=False,
    ).astype(jnp.bfloat16)
    fed = jnp.dot(hidden, full_down, preferred_element_type=jnp.float32).astype(jnp.bfloat16)
    second = reduce_norm(fed.reshape(split), first, gain_second, shift_second, False, 3)
    back = pick(jnp.maximum(got_slots, 0), second)
    [returned] = swap(back.reshape(n_data, slots_per, rows, width), n_mp, 4)
    mixed = pick(position, returned.reshape(buffer_rows, page, width))
    kv_cache = jnp.stack([keys, values], axis=1)
    return (mixed.reshape(pages_dev * page, width), kv_cache)


def solution(mesh):
    return jax.shard_map(
        body,
        mesh=mesh,
        in_specs=(
            P("dp", None),
            P("dp"),
            P("dp"),
            P("dp", "mp"),
            P("dp", "mp"),
            P("dp", "mp"),
            P("mp", "dp"),
            P("dp", "mp"),
            P("mp", "dp"),
            P(),
            P(),
            P(),
            P(),
        ),
        out_specs=(P("dp", None), P("dp", None, "mp")),
        check_vma=False,
    )
```

time: 650 us -> 342 us (0.53)
  Pallas kernels: 0 us -> 269 us
  waiting for transfers between devices: 258 us -> 1.38 us
  blocking collectives: 204 us -> 0 us
  matrix products: 60.6 us -> 25.8 us
  other arithmetic: 36.5 us -> 3.84 us
  local copies, waits for them, and re-layouts: 45.5 us -> 22.1 us
  starting transfers between devices: 22.4 us -> 0.08 us
    pallas_call x0 -> x9, Pallas kernels: none -> 269 us  [the longest x2 128 us: swap(): pl.pallas_call(functools.partial(swap_kernel, n_dp, n_mp, with_extra), ou...]
    all_gather x4 -> x0, blocking collectives: 204 us -> none  [the longest x1 113 us: body(): lax.all_gather(w_key, 'dp', axis=0, tiled=True)]
    psum x2 -> x0, waiting for transfers between devices: 149 us -> none  [finish(): lax.psum(partial_value.astype(jnp.bfloat16), 'mp').astype(jnp.float32)]
    all_to_all x4 -> x0, waiting for transfers between devices: 93.4 us -> none  [the longest x1 88.2 us: body(): lax.all_to_all(outgoing_pages(second, got_slots, pages_dev, page), 'dp',...]
    dot_general x20 -> x0, matrix products: 34.6 us -> none  [the longest x8 12.2 us: per_block(): jnp.dot(attn_weights, values, preferred_element_type=jnp.float32)]
    all_to_all x4 -> x0, starting transfers between devices: 22.2 us -> none  [the longest x1 7.28 us: body(): lax.all_to_all(send_slots, 'dp', split_axis=0, concat_axis=0, tiled=True)]
    reduce_sum x13 -> x4, other arithmetic: 21.8 us -> 0.43 us  [the longest x1 0.11 us: body(): jnp.sum(jnp.where(placed, local_slot[None, :] + 1, 0), axis=1) - 1]
    gather x4 -> x0, local copies, waits for them, and re-layouts: 15.1 us -> none  [the longest x1 4.86 us: body(): dealt = got_pages[source_row].reshape(pages_dev * page, got_pages.shape[2])]
  transfers between devices with their start and end apart: 8 -> 2, of which waited for: 5 -> 0; matrix products, arithmetic and copies ran while one was open for 5% -> 6% of each run, Pallas kernels for 0% -> 54%
where the time goes in v1:
time: 342 us; the launch traced here: 336 us
  Pallas kernels  269 us (79%)
  matrix products  25.8 us (8%)
  local copies, waits for them, and re-layouts  22.1 us (6%)
  between operations  14.2 us (4%)
  other arithmetic  3.84 us (1%)
    pallas_call x2, Pallas kernels, swap(): pl.pallas_call(functools.partial(swap_kernel, n_dp, n_mp, with_extra), ou...  128 us
    pallas_call x2, Pallas kernels, reduce_norm(): pl.pallas_call(functools.partial(reduce_kernel, n_mp, chunk, gather), out...  72 us
    pallas_call x3, Pallas kernels, pick(): pl.pallas_call(pick_kernel, out_shape=jax.ShapeDtypeStruct((count, *out_b...  28.8 us
    pallas_call x1, Pallas kernels, attend(): pl.pallas_call(attend_kernel, out_shape=jax.ShapeDtypeStruct((tokens, fea...  28.4 us
    dot_general x1, matrix products, body(): jnp.dot(hidden, full_down, preferred_element_type=jnp.float32)  25.8 us
    unnamed x31, local copies, waits for them, and re-layouts  20.2 us
    pallas_call x1, Pallas kernels, project(): pl.pallas_call(project_kernel, out_shape=[jax.ShapeDtypeStruct((count, pa...  11.3 us
  transfers between devices with their start and end apart: 2, of which 0 were waited for; matrix products, arithmetic and copies ran while one was open for 6% of the time, Pallas kernels for 54%

profile of v1, /device:TPU:0, one launch (start us, length us, event | category | flops | bytes accessed | tf_op | source)
XLA Modules:
  0.0 336.3 jit_solution(1610946491865696168)
XLA Ops:
  7.2 0.0 copy-start.11
  7.2 0.0 copy-start.10
  7.2 0.0 copy-start.9
  7.2 0.0 copy-start.8
  7.2 0.0 all-gather.3.cloned.1.call-start
  7.3 0.7 all-gather.3.cloned.1.call-update
  7.9 0.0 all-gather.5.cloned.1.call-start
  8.0 0.7 all-gather.5.cloned.1.call-update
  8.7 0.7 fusion.12
  9.4 0.1 convert_reduce_fusion
  9.5 0.1 select_reduce_fusion.3
  9.6 0.1 sub.11
  9.7 0.1 copy.22
  9.8 0.9 copy.23
  10.7 0.6 pad_add_fusion.1.rows_ref
  11.3 9.5 %pick.3 = bf16[16,1,32,1024]{3,2,1,0:T(8,128)(2,1)} custom-call(s32[17]{0:T(128)} %pad_add_fusion.1.rows_ref, bf16[14,4,32,1024]{3,2,1,0:T(8,128)(2,1)} %bitcast.55), custom_call_target="tpu_custom_call" | custom-call | tf_op jit(solution)/shard_map/pick/pallas_call | solution.py:304
  20.9 0.0 copy-done.11
  20.9 0.1 select_reduce_fusion.1
  21.0 0.1 broadcast_in_dim.100
  21.1 0.6 pad_add_fusion.refs_1_
  21.7 0.0 copy-done.10
  21.7 0.0 copy-done.9
  21.7 0.0 copy-done.8
  21.7 0.7 pad_maximum_fusion.1.refs_2_
  22.4 85.6 %swap_1.1 = (bf16[8,2,4,32,1024]{4,3,2,1,0:T(8,128)(2,1)}, s32[8,2,8,128]{3,2,1,0:T(8,128)}, bf16[8,128,1024]{2,1,0:T(8,128)(2,1)}) custom-call(bf16[8,2,32,1024]{3,2,1,0:T(8,128)(2,1)} %bitcast.52, s32[8,2,8,128]{3,2,1,0:T(8,128)} %pad_add_fusion.refs_1_, bf16[128,1024]{1,0:T(8,128)(2,1)} %pad_maximum_fusion.1.refs_2_), custom_call_target="tpu_custom_call" | custom-call | tf_op jit(solution)/shard_map/swap_1/pallas_call | solution.py:141
  108.0 0.8 slice.8
  108.9 0.8 slice.9
  109.7 0.1 copy.27
  109.8 0.1 select_reduce_fusion
  109.9 0.3 copy.29
  110.3 0.1 select_reduce_fusion.2.rows_ref
  110.4 1.6 copy-done.1
  112.0 11.3 %project.1 = (bf16[14,128,1024]{2,1,0:T(8,128)(2,1)}, bf16[1792,256]{1,0:T(8,128)(2,1)S(1)}, bf16[1792,256]{1,0:T(8,128)(2,1)S(1)}, bf16[1792,256]{1,0:T(8,128)(2,1)S(1)}) custom-call(s32[14]{0:T(128)S(1)} %select_reduce_fusion.2.rows_ref, bf16[16,128,1024]{2,1,0:T(8,128)(2,1)} %bitcast.54, bf16[1024,1024]{1,0:T(8,128)(2,1)S(1)} %bitcast.38), custom_call_target="tpu_custom_call" | custom-call | tf_op jit(solution)/shard_map/project/pallas_call | solution.py:333
  123.2 0.2 pad_maximum_fusion
  123.4 12.4 %copy.26 = bf16[1792,2,256]{2,1,0:T(2,128)(2,1)} copy(bf16[1792,2,256]{2,0,1:T(8,128)(2,1)S(1)} %pad_maximum_fusion) | data formatting | bytes 3670016
  135.8 28.4 %attend.1 = bf16[1792,1024]{1,0:T(8,128)(2,1)} custom-call(bf16[1792,256]{1,0:T(8,128)(2,1)S(1)} %get-tuple-element.12.query, bf16[1792,256]{1,0:T(8,128)(2,1)S(1)} %get-tuple-element.13.keys, bf16[1792,256]{1,0:T(8,128)(2,1)S(1)} %get-tuple-element.14.values, s32[1792,1]{1,0:T(8,128)S(1)} %bitcast.42, s32[1,1792]{1,0:T(1,128)S(1)} %bitcast.45, ...), custom_call_target="tpu_custom_call" | custom-call | tf_op jit(solution)/shard_map/attend/pallas_call | solution.py:387
  164.2 47.4 %reduce_2.1.refs_1_ = bf16[14,4,32,1024]{3,2,1,0:T(8,128)(2,1)S(1)} custom-call(bf16[14,4,32,1024]{3,2,1,0:T(8,128)(2,1)} %bitcast.51, bf16[14,4,32,1024]{3,2,1,0:T(8,128)(2,1)} %bitcast.57, f32[1,1,1024]{2,1,0:T(1,128)S(1)} %bitcast.46, f32[1,1,1024]{2,1,0:T(1,128)S(1)} %bitcast.47), custom_call_target="tpu_custom_call" | custom-call | tf_op jit(solution)/shard_map/reduce_2/pallas_call | solution.py:268
  211.6 0.0 copy-start
  211.6 1.8 copy-done
  213.5 0.5 broadcast_maximum_fusion.rows_ref
  214.0 25.8 %convolution_convert_fusion = bf16[1792,1024]{1,0:T(8,128)(2,1)} fusion(bf16[1024,1024]{1,0:T(8,128)(2,1)} %all-gather.5.cloned.1.call-done, bf16[1792,1024]{1,0:T(8,128)(2,1)} %bitcast.37, bf16[1024,1024]{1,0:T(8,128)(2,1)} %all-gather.3.cloned.1.call-done), kind=kOutput, calls=%fused_computation.19 | convolution fusion | flops 7637303296 | bytes 11534336 | tf_op jit(solution)/shard_map/dot_general | solution.py:470
  239.8 0.0 copy-done.7
  239.8 2.0 copy-done.3
  241.9 24.6 %reduce_3.1.src = bf16[14,32,1024]{2,1,0:T(8,128)(2,1)S(1)} custom-call(bf16[14,4,32,1024]{3,2,1,0:T(8,128)(2,1)S(1)} %bitcast.43, bf16[14,4,32,1024]{3,2,1,0:T(8,128)(2,1)} %copy-done, f32[1,1,1024]{2,1,0:T(1,128)S(1)} %bitcast.48, f32[1,1,1024]{2,1,0:T(1,128)S(1)} %bitcast.49), custom_call_target="tpu_custom_call" | custom-call | tf_op jit(solution)/shard_map/reduce_3/pallas_call | solution.py:268
  266.5 0.9 copy-done.2
  267.4 9.5 %pick.4 = bf16[16,32,1024]{2,1,0:T(8,128)(2,1)} custom-call(s32[16]{0:T(128)} %broadcast_maximum_fusion.rows_ref, bf16[14,32,1024]{2,1,0:T(8,128)(2,1)} %copy-done.2), custom_call_target="tpu_custom_call" | custom-call | tf_op jit(solution)/shard_map/pick/pallas_call | solution.py:304
  276.9 42.8 %swap_4.1 = bf16[8,2,4,32,1024]{4,3,2,1,0:T(8,128)(2,1)} custom-call(bf16[8,2,32,1024]{3,2,1,0:T(8,128)(2,1)} %bitcast.53), custom_call_target="tpu_custom_call" | custom-call | tf_op jit(solution)/shard_map/swap_4/pallas_call | solution.py:141
  319.8 9.7 %pick.5 = bf16[14,128,1024]{2,1,0:T(8,128)(2,1)} custom-call(s32[14]{0:T(128)} %copy-done.12, bf16[16,128,1024]{2,1,0:T(8,128)(2,1)} %bitcast.50), custom_call_target="tpu_custom_call" | custom-call | tf_op jit(solution)/shard_map/pick/pallas_call | solution.py:304
  (19 shorter events, 0.1 us)
Async XLA Ops:
  7.2 13.7 %copy-start.11 = (s32[1792]{0:T(1024)S(1)}, s32[1792]{0:T(1024)}, u32[]{:S(2)}) copy-start(s32[1792]{0:T(1024)} %param.14) | copy-start | bytes 21508
  7.2 14.5 %copy-start.10 = (bf16[128,256]{1,0:T(8,128)(2,1)S(1)}, bf16[128,256]{1,0:T(8,128)(2,1)}, u32[]{:S(2)}) copy-start(bf16[128,256]{1,0:T(8,128)(2,1)} %param.16) | copy-start | bytes 196612
  7.2 14.5 %copy-start.9 = (bf16[128,256]{1,0:T(8,128)(2,1)S(1)}, bf16[128,256]{1,0:T(8,128)(2,1)}, u32[]{:S(2)}) copy-start(bf16[128,256]{1,0:T(8,128)(2,1)} %param.17) | copy-start | bytes 196612
  7.2 14.5 %copy-start.8 = (bf16[128,256]{1,0:T(8,128)(2,1)S(1)}, bf16[128,256]{1,0:T(8,128)(2,1)}, u32[]{:S(2)}) copy-start(bf16[128,256]{1,0:T(8,128)(2,1)} %param.18) | copy-start | bytes 196612
  7.2 206.7 %all-gather.3.cloned.1.call-start = ((), (), s32[]{:S(2)}) async-start(), calls=%async_computation | async-start | bytes 2359296 | tf_op jit(solution)/shard_map/all_gather | solution.py:452
  7.9 206.0 %all-gather.5.cloned.1.call-start = ((), (), s32[]{:S(2)}) async-start(), calls=%async_computation.1 | async-start | bytes 2359296 | tf_op jit(solution)/shard_map/all_gather | solution.py:453
  9.5 113.8 %copy-start.12 = (s32[14]{0:T(128)}, s32[14]{0:T(128)S(1)}, u32[]{:S(2)}) copy-start(s32[14]{0:T(128)S(1)} %multiply_add_fusion.rows_ref) | copy-start | bytes 172
  110.4 1.6 copy-start.1
  135.8 28.4 %copy-start.4 = (f32[1024]{0:T(1024)S(1)}, f32[1024]{0:T(1024)}, u32[]{:S(2)}) copy-start(f32[1024]{0:T(1024)} %param.22) | copy-start | bytes 12292
  135.8 28.4 %copy-start.5 = (f32[1024]{0:T(1024)S(1)}, f32[1024]{0:T(1024)}, u32[]{:S(2)}) copy-start(f32[1024]{0:T(1024)} %param.23) | copy-start | bytes 12292
  211.6 1.8 copy-start
  214.0 25.9 %copy-start.6 = (f32[1024]{0:T(1024)S(1)}, f32[1024]{0:T(1024)}, u32[]{:S(2)}) copy-start(f32[1024]{0:T(1024)} %param.24) | copy-start | bytes 12292
  214.0 25.9 %copy-start.7 = (f32[1024]{0:T(1024)S(1)}, f32[1024]{0:T(1024)}, u32[]{:S(2)}) copy-start(f32[1024]{0:T(1024)} %param.25) | copy-start | bytes 12292
  239.8 2.0 copy-start.3
  266.5 0.9 copy-start.2
Sparse Core Ops, SparseCore 0:
  10.2 79.6 all-gather.2
  91.9 55.3 all-gather.4

commit v2 on v1

v2 whole, which is shorter than its diff:
```python
import functools

import jax
import jax.numpy as jnp
from jax import lax
from jax.experimental import pallas as pl
from jax.experimental.pallas import tpu as pltpu
from jax.sharding import PartitionSpec as P

HEAD = 64
MESH = pl.DeviceIdType.MESH
VMEM_BYTES = 48 * 1024 * 1024


def mp_peers(me_m, n_mp):
    return me_m + 1 - 2 * lax.rem(me_m, 2), lax.rem(me_m + 2, n_mp)


def swap_kernel(n_dp, n_mp, with_extra, *refs):
    if with_extra:
        send, meta, weight, recv, got_meta, full, *sems = refs
    else:
        send, recv, *sems = refs
    local, a_send, a_recv, f_send, f_recv, *more = sems
    me_d, me_m = lax.axis_index("dp"), lax.axis_index("mp")
    sib, far = mp_peers(me_m, n_mp)
    barrier = pltpu.get_barrier_semaphore()
    for k in range(1, n_dp):
        pl.semaphore_signal(
            barrier, inc=1, device_id=(lax.rem(me_d + k, n_dp), me_m), device_id_type=MESH
        )
    for peer in (sib, far):
        pl.semaphore_signal(barrier, inc=1, device_id=(me_d, peer), device_id_type=MESH)
    pl.semaphore_wait(barrier, n_dp + 1)

    def remote(src, dst, s_sem, r_sem, dev):
        return pltpu.make_async_remote_copy(
            src_ref=src,
            dst_ref=dst,
            send_sem=s_sem,
            recv_sem=r_sem,
            device_id=dev,
            device_id_type=MESH,
        )

    def source(k):
        return lax.rem(me_d - k + n_dp, n_dp)

    own = pltpu.make_async_copy(send.at[me_d], recv.at[me_d, :, me_m], local.at[0])
    own.start()
    outs = []
    if with_extra:
        m_send, m_recv, z_send, z_recv, y_send, y_recv = more
        own_meta = pltpu.make_async_copy(meta.at[me_d], got_meta.at[me_d], local.at[1])
        own_meta.start()
        own_w = pltpu.make_async_copy(weight, full.at[me_d], local.at[2])
        own_w.start()
        for k in range(1, n_dp):
            to = lax.rem(me_d + k, n_dp)
            outs.append(
                remote(meta.at[to], got_meta.at[me_d], m_send.at[k], m_recv.at[k], (to, me_m))
            )
            outs[-1].start()
    slots = send.shape[1]
    for slot in range(slots):
        for k in range(1, n_dp):
            to = lax.rem(me_d + k, n_dp)
            outs.append(
                remote(
                    send.at[to, slot],
                    recv.at[me_d, slot, me_m],
                    a_send.at[slot, k],
                    a_recv.at[slot, k],
                    (to, me_m),
                )
            )
            outs[-1].start()
    if with_extra:
        rows = n_dp // 2
        b = lax.rem(me_d, 2)
        a = (me_d - b) // 2
        across = me_d + 1 - 2 * b
        outs.append(remote(weight, full.at[me_d], y_send.at[0], y_recv.at[0], (me_d + 1 - 2 * b, me_m)))
        outs[-1].start()
        for k in range(1, rows):
            to = lax.rem(a + k, rows) * 2 + b
            outs.append(remote(weight, full.at[me_d], z_send.at[k], z_recv.at[k], (to, me_m)))
            outs[-1].start()

    def copy_on(way, slot, k, quarter):
        block = recv.at[source(k), slot, quarter]
        peer = far if way == 0 else sib
        return remote(
            block, block, f_send.at[way, slot, k], f_recv.at[way, slot, k], (me_d, peer)
        )

    def hand_on(slot, k):
        for way in (0, 1):
            outs.append(copy_on(way, slot, k, me_m))
            outs[-1].start()

    def hand_far(slot, k):
        copy_on(0, slot, k, far).wait_recv()
        outs.append(copy_on(2, slot, k, far))
        outs[-1].start()

    own.wait()
    for slot in range(slots):
        hand_on(slot, 0)
    for slot in range(slots):
        for k in range(1, n_dp):
            block = recv.at[source(k), slot, me_m]
            remote(block, block, a_send.at[slot, k], a_recv.at[slot, k], (me_d, far)).wait_recv()
            hand_on(slot, k)
            hand_far(slot, k - 1)
        hand_far(slot, n_dp - 1)
    if with_extra:
        for k in range(1, rows):
            block = full.at[lax.rem(a - k + rows, rows) * 2 + b]
            remote(block, block, z_send.at[k], z_recv.at[k], (across, me_m)).wait_recv()
            outs.append(remote(block, block, y_send.at[k], y_recv.at[k], (across, me_m)))
            outs[-1].start()
        for k in range(rows):
            block = full.at[lax.rem(a - k + rows, rows) * 2 + 1 - b]
            remote(block, block, y_send.at[k], y_recv.at[k], (across, me_m)).wait_recv()
        for k in range(1, n_dp):
            block = got_meta.at[source(k)]
            remote(block, block, m_send.at[k], m_recv.at[k], (across, me_m)).wait_recv()
        own_meta.wait()
        own_w.wait()
    sib_far = lax.rem(sib + 2, n_mp)
    for slot in range(slots):
        for k in range(n_dp):
            copy_on(1, slot, k, sib).wait_recv()
            copy_on(2, slot, k, sib_far).wait_recv()
    for copy in outs:
        copy.wait_send()


def swap(send, n_mp, collective_id, meta=None, weight=None):
    n_dp, slots, rows, width = send.shape
    with_extra = meta is not None
    any_spec = pl.BlockSpec(memory_space=pl.ANY)
    outs = [jax.ShapeDtypeStruct((n_dp, slots, n_mp, rows, width), send.dtype)]
    sems = [(3,)] + [(slots, n_dp)] * 2 + [(3, slots, n_dp)] * 2
    args = [send]
    if with_extra:
        outs += [
            jax.ShapeDtypeStruct(meta.shape, meta.dtype),
            jax.ShapeDtypeStruct((n_dp, *weight.shape), weight.dtype),
        ]
        sems += [(n_dp,), (n_dp,)] + [(n_dp // 2,)] * 4
        args += [meta, weight]
    return pl.pallas_call(
        functools.partial(swap_kernel, n_dp, n_mp, with_extra),
        out_shape=outs,
        in_specs=[any_spec] * len(args),
        out_specs=[any_spec] * len(outs),
        scratch_shapes=[pltpu.SemaphoreType.DMA(s) for s in sems],
        compiler_params=pltpu.CompilerParams(collective_id=collective_id, has_side_effects=True),
        name=f"swap_{collective_id}",
    )(*args)


def pick_kernel(count, part, table, src, out, sem):
    copies = []
    for i in range(count):
        block = src.at[table[i]]
        if part:
            block = block.at[table[count]]
        copies.append(pltpu.make_async_copy(block, out.at[i], sem.at[i]))
        copies[-1].start()
    for copy in copies:
        copy.wait()


def pick(table, source, part=None):
    count = table.shape[0]
    shape = source.shape[1:] if part is None else source.shape[2:]
    scalars = table if part is None else jnp.concatenate([table, part.reshape(1)])
    any_spec = pl.BlockSpec(memory_space=pl.ANY)
    return pl.pallas_call(
        functools.partial(pick_kernel, count, part is not None),
        out_shape=jax.ShapeDtypeStruct((count, *shape), source.dtype),
        in_specs=[pl.BlockSpec(memory_space=pltpu.SMEM), any_spec],
        out_specs=any_spec,
        scratch_shapes=[pltpu.SemaphoreType.DMA((count,))],
        name="pick",
    )(scalars, source)


def project_kernel(table, src, weight, dealt, query, keys, values, pages, w_held, sem):
    count, page, width = pages.shape
    cols = query.shape[1]
    n_mp, rows = src.shape[1], src.shape[2]
    w_copy = pltpu.make_async_copy(weight, w_held, sem.at[2 * count])
    w_copy.start()
    copies, quarters = [], []
    for i in range(count):
        block = src.at[table[i]]
        copies.append(
            pltpu.make_async_copy(block, pages.at[i].reshape(n_mp, rows, width), sem.at[i])
        )
        copies[-1].start()
        quarters.append(
            pltpu.make_async_copy(block.at[table[count]], dealt.at[i], sem.at[count + i])
        )
        quarters[-1].start()
    w_copy.wait()
    group = 2 if count % 2 == 0 else 1
    for i in range(0, count, group):
        for k in range(group):
            copies[i + k].wait()
        held = pages[i : i + group].reshape(group * page, width)
        both = jnp.dot(held, w_held[:, : 3 * cols], preferred_element_type=jnp.float32)
        at = pl.ds(i * page, group * page)
        query[at] = both[:, :cols].astype(query.dtype)
        keys[at] = both[:, cols : 2 * cols].astype(keys.dtype)
        values[at] = both[:, 2 * cols :].astype(values.dtype)
    for copy in quarters:
        copy.wait()


def project(source_row, me_m, got, weight):
    count = source_row.shape[0]
    _, n_mp, rows, width = got.shape
    page = n_mp * rows
    cols = weight.shape[1] // 4
    flat = jax.ShapeDtypeStruct((count * page, cols), got.dtype)
    any_spec = pl.BlockSpec(memory_space=pl.ANY)
    vmem = pl.BlockSpec(memory_space=pltpu.VMEM)
    return pl.pallas_call(
        project_kernel,
        out_shape=[jax.ShapeDtypeStruct((count, rows, width), got.dtype), flat, flat, flat],
        in_specs=[pl.BlockSpec(memory_space=pltpu.SMEM), any_spec, any_spec],
        out_specs=[any_spec, vmem, vmem, vmem],
        scratch_shapes=[
            pltpu.VMEM((count, page, width), got.dtype),
            pltpu.VMEM(weight.shape, weight.dtype),
            pltpu.SemaphoreType.DMA((2 * count + 1,)),
        ],
        compiler_params=pltpu.CompilerParams(vmem_limit_bytes=VMEM_BYTES),
        name="project",
    )(jnp.concatenate([source_row, me_m.reshape(1)]), got, weight)


def attend_rows(at, query, keys, values, row_ids, col_ids, weight):
    width = query.shape[1]
    lane = lax.broadcasted_iota(jnp.int32, (1, width), 1)
    same = row_ids[at] == col_ids[...]
    rows = query[at].astype(jnp.float32) * HEAD**-0.5
    context = jnp.zeros(rows.shape, jnp.float32)
    for head in range(width // HEAD):
        here = (lane >= head * HEAD) & (lane < (head + 1) * HEAD)
        picked = jnp.where(here, rows, 0.0).astype(query.dtype)
        scores = lax.dot_general(
            picked, keys[...], (((1,), (1,)), ((), ())), preferred_element_type=jnp.float32
        )
        scores = jnp.where(same, scores, -1e30)
        raised = jnp.exp(scores - jnp.max(scores, axis=1, keepdims=True))
        total = jnp.sum(raised, axis=1, keepdims=True)
        mixed = jnp.dot(
            raised.astype(values.dtype), values[...], preferred_element_type=jnp.float32
        )
        context = jnp.where(here, mixed / total, context)
    return lax.dot_general(
        context.astype(query.dtype),
        weight[...],
        (((1,), (1,)), ((), ())),
        preferred_element_type=jnp.float32,
    )


def feed_rows(chunk, first, w_up, w_down):
    pages, n_mp, rows, width = first.shape
    raised = jnp.dot(
        first[chunk].reshape(-1, width), w_up[...], preferred_element_type=jnp.float32
    )
    hidden = 0.5 * raised * (1.0 + lax.erf(raised * 0.5**0.5))
    return jnp.dot(hidden.astype(first.dtype), w_down[...], preferred_element_type=jnp.float32)


def reduce_kernel(n_mp, chunk, gather, *refs):
    n_work = 6 if gather else 3
    work, refs = refs[:n_work], refs[n_work:]
    resid, gain, shift, out, part, sib_in, acc, far_in, res, *sems = refs
    local, s_send, s_recv, x_send, x_recv, *more = sems
    me_d, me_m = lax.axis_index("dp"), lax.axis_index("mp")
    sib, far = mp_peers(me_m, n_mp)
    sib_far = lax.rem(sib + 2, n_mp)
    chunks = part.shape[0] // chunk
    barrier = pltpu.get_barrier_semaphore()
    for peer in (sib, far):
        pl.semaphore_signal(barrier, inc=1, device_id=(me_d, peer), device_id_type=MESH)
    pl.semaphore_wait(barrier, 2)
    own = pltpu.make_async_copy(resid if gather else resid.at[:, me_m], res, local.at[0])
    own.start()

    def at(c):
        return pl.ds(c * chunk, chunk)

    def to_sib(half, c):
        quarter = sib_far if half == 0 else sib
        return pltpu.make_async_remote_copy(
            src_ref=part.at[at(c), quarter],
            dst_ref=sib_in.at[half, at(c)],
            send_sem=s_send.at[half, c],
            recv_sem=s_recv.at[half, c],
            device_id=(me_d, sib),
            device_id_type=MESH,
        )

    def to_far(c):
        return pltpu.make_async_remote_copy(
            src_ref=acc.at[at(c)],
            dst_ref=far_in.at[at(c)],
            send_sem=x_send.at[c],
            recv_sem=x_recv.at[c],
            device_id=(me_d, far),
            device_id_type=MESH,
        )

    def spread(way, c, quarter):
        g_send, g_recv = more
        block = out.at[at(c), quarter]
        return pltpu.make_async_remote_copy(
            src_ref=block,
            dst_ref=block,
            send_sem=g_send.at[way, c],
            recv_sem=g_recv.at[way, c],
            device_id=(me_d, far if way == 0 else sib),
            device_id_type=MESH,
        )

    def produce(c):
        if gather:
            tall = chunk * part.shape[1] * part.shape[2]
            made = attend_rows(pl.ds(pl.multiple_of(c * tall, tall), tall), *work)
        else:
            made = feed_rows(at(c), *work)
        part[at(c)] = made.astype(part.dtype).reshape(chunk, *part.shape[1:])
        to_sib(0, c).start()
        to_sib(1, c).start()

    def add_far(c):
        to_sib(0, c).wait_recv()
        mine = part[at(c), far].astype(jnp.float32) + sib_in[0, at(c)].astype(jnp.float32)
        acc[at(c)] = mine.astype(acc.dtype)
        to_far(c).start()

    def settle(c):
        to_sib(1, c).wait_recv()
        to_far(c).wait_recv()
        total = (
            part[at(c), me_m].astype(jnp.float32)
            + sib_in[1, at(c)].astype(jnp.float32)
            + far_in[at(c)].astype(jnp.float32)
            + res[at(c)].astype(jnp.float32)
        )
        center = total - jnp.mean(total, axis=-1, keepdims=True)
        spread_sq = jnp.mean(center * center, axis=-1, keepdims=True)
        normed = center * lax.rsqrt(spread_sq + 1e-05) * gain[...] + shift[...]
        if gather:
            out[at(c), me_m] = normed.astype(out.dtype)
            spread(0, c, me_m).start()
            spread(1, c, me_m).start()
        else:
            out[at(c)] = normed.astype(out.dtype)

    produce(0)
    own.wait()

    def step(c, _):
        produce(c)
        add_far(c - 1)

        @pl.when(c >= 3)
        def _():
            settle(c - 3)

        return 0

    lax.fori_loop(1, chunks, step, 0)
    add_far(chunks - 1)
    for c in range(max(chunks - 3, 0), chunks):
        settle(c)
    if gather:

        def pass_on(c, _):
            spread(0, c, far).wait_recv()
            spread(2, c, far).start()
            return 0

        lax.fori_loop(0, chunks, pass_on, 0)
        for c in range(chunks):
            spread(1, c, sib).wait_recv()
            spread(2, c, sib_far).wait_recv()
            for way, quarter in ((0, me_m), (1, me_m), (2, far)):
                spread(way, c, quarter).wait_send()
    for c in range(chunks):
        to_sib(0, c).wait_send()
        to_sib(1, c).wait_send()
        to_far(c).wait_send()


def reduce_norm(work, split, resid, gain, shift, gather, collective_id):
    pages, n_mp, rows, width = split
    chunk = 2 if pages % 2 == 0 else 1
    chunks = pages // chunk
    quarter = (pages, rows, width)
    dtype = resid.dtype
    vmem = pl.BlockSpec(memory_space=pltpu.VMEM)
    out_shape = split if gather else quarter
    sems = [(1,), (2, chunks), (2, chunks), (chunks,), (chunks,)]
    if gather:
        sems += [(3, chunks), (3, chunks)]
    return pl.pallas_call(
        functools.partial(reduce_kernel, n_mp, chunk, gather),
        out_shape=jax.ShapeDtypeStruct(out_shape, dtype),
        in_specs=[vmem] * len(work) + [pl.BlockSpec(memory_space=pl.ANY), vmem, vmem],
        out_specs=vmem,
        scratch_shapes=[
            pltpu.VMEM(split, dtype),
            pltpu.VMEM((2, *quarter), dtype),
            pltpu.VMEM(quarter, dtype),
            pltpu.VMEM(quarter, dtype),
            pltpu.VMEM(quarter, dtype),
        ]
        + [pltpu.SemaphoreType.DMA(s) for s in sems],
        compiler_params=pltpu.CompilerParams(
            collective_id=collective_id, has_side_effects=True, vmem_limit_bytes=VMEM_BYTES
        ),
        name=f"reduce_{collective_id}",
    )(*work, resid, gain.reshape(1, 1, width), shift.reshape(1, 1, width))


def body(
    tokens,
    segment_ids,
    page_table,
    w_query,
    w_key,
    w_value,
    w_out,
    w_up,
    w_down,
    gain_first,
    shift_first,
    gain_second,
    shift_second,
):
    n_data, n_mp = lax.axis_size("dp"), lax.axis_size("mp")
    me_m = lax.axis_index("mp").astype(jnp.int32)
    pages_dev = page_table.shape[0]
    page = tokens.shape[0] // pages_dev
    width = tokens.shape[1]
    rows = page // n_mp
    slots_per = (pages_dev + n_data - 1) // n_data
    buffer_rows = n_data * slots_per
    target = page_table // pages_dev
    local_slot = page_table % pages_dev
    order = jnp.arange(pages_dev, dtype=jnp.int32)
    earlier = (target[:, None] == target[None, :]) & (order[:, None] < order[None, :])
    rank = jnp.sum(earlier.astype(jnp.int32), axis=0)
    position = target * slots_per + rank
    places = jnp.arange(buffer_rows, dtype=jnp.int32)
    placed = position[None, :] == places[:, None]
    page_of = jnp.sum(jnp.where(placed, order[None, :], 0), axis=1)
    ids_paged = segment_ids.reshape(pages_dev, page)
    send_ids = jnp.sum(jnp.where(placed[:, :, None], ids_paged[None], 0), axis=1)
    send_slots = jnp.sum(jnp.where(placed, local_slot[None, :] + 1, 0), axis=1) - 1
    meta = jnp.concatenate(
        [
            send_ids[:, None, :],
            jnp.broadcast_to(send_slots[:, None, None], (buffer_rows, 7, page)),
        ],
        axis=1,
    ).reshape(n_data, slots_per, 8, page)
    weight = jnp.concatenate([w_query, w_key, w_value, w_out.T], axis=1)
    send = pick(page_of, tokens.reshape(pages_dev, n_mp, rows, width), me_m)
    got, got_meta, full = swap(
        send.reshape(n_data, slots_per, rows, width), n_mp, 1, meta, weight
    )
    w_up, w_down, got_meta = lax.optimization_barrier((w_up, w_down, got_meta))
    full_up = lax.all_gather(w_up, "dp", axis=0, tiled=True)
    full_down = lax.all_gather(w_down, "dp", axis=1, tiled=True)
    full = full.reshape(width, weight.shape[1])
    got_meta = got_meta.reshape(buffer_rows, 8, page)
    got_slots = got_meta[:, 1, 0]
    matches = got_slots[None, :] == order[:, None]
    source_row = jnp.sum(jnp.where(matches, places[None, :], 0), axis=1)
    dealt_ids = jnp.sum(jnp.where(matches[:, :, None], got_meta[None, :, 0, :], 0), axis=1)
    dealt, query, keys, values = project(
        source_row, me_m, got.reshape(buffer_rows, n_mp, rows, width), full
    )
    split = (pages_dev, n_mp, rows, width)
    ids = dealt_ids.reshape(-1)
    attending = (query, keys, values, ids.reshape(-1, 1), ids.reshape(1, -1), full[:, -query.shape[1] :])
    first = reduce_norm(attending, split, dealt, gain_first, shift_first, True, 2)
    feeding = (first, full_up, full_down)
    second = reduce_norm(feeding, split, first, gain_second, shift_second, False, 3)
    back = pick(jnp.maximum(got_slots, 0), second)
    [returned] = swap(back.reshape(n_data, slots_per, rows, width), n_mp, 4)
    mixed = pick(position, returned.reshape(buffer_rows, page, width))
    kv_cache = jnp.stack([keys, values], axis=1)
    return (mixed.reshape(pages_dev * page, width), kv_cache)


def solution(mesh):
    return jax.shard_map(
        body,
        mesh=mesh,
        in_specs=(
            P("dp", None),
            P("dp"),
            P("dp"),
            P("dp", "mp"),
            P("dp", "mp"),
            P("dp", "mp"),
            P("mp", "dp"),
            P("dp", "mp"),
            P("mp", "dp"),
            P(),
            P(),
            P(),
            P(),
        ),
        out_specs=(P("dp", None), P("dp", None, "mp")),
        check_vma=False,
    )
```

time: 342 us -> 447 us (1.31)
  Pallas kernels: 269 us -> 381 us
  matrix products: 25.8 us -> 0 us
  waiting for transfers between devices: 1.38 us -> 23.4 us
    pallas_call x5 -> x4, Pallas kernels: 68.4 us -> 187 us  [the longest x3 181 us: pick(): pl.pallas_call(functools.partial(pick_kernel, count, part is not None), o...]
    dot_general x1 -> x0, matrix products: 25.8 us -> none  [body(): jnp.dot(hidden, full_down, preferred_element_type=jnp.float32)]
    all_gather x1, waiting for transfers between devices: 0.01 us -> 22.7 us  [body(): full_down = lax.all_gather(w_down, 'dp', axis=1, tiled=True)]
    pallas_call x2, Pallas kernels: 128 us -> 109 us  [swap(): pl.pallas_call(functools.partial(swap_kernel, n_dp, n_mp, with_extra), ou...]
    pallas_call x2, Pallas kernels: 72 us -> 84.6 us  [reduce_norm(): pl.pallas_call(functools.partial(reduce_kernel, n_mp, chunk, gather), out...]
  transfers between devices with their start and end apart: 2 -> 2, of which waited for: 0 -> 1; matrix products, arithmetic and copies ran while one was open for 6% -> 4% of each run, Pallas kernels for 54% -> 14%
where the time goes in v2:
time: 447 us; the launch traced here: 444 us
  Pallas kernels  381 us (85%)
  waiting for transfers between devices  23.4 us (5%)
  local copies, waits for them, and re-layouts  21 us (5%)
  between operations  14.2 us (3%)
    pallas_call x3, Pallas kernels, pick(): pl.pallas_call(functools.partial(pick_kernel, count, part is not None), o...  181 us
    pallas_call x2, Pallas kernels, swap(): pl.pallas_call(functools.partial(swap_kernel, n_dp, n_mp, with_extra), ou...  109 us
    pallas_call x2, Pallas kernels, reduce_norm(): pl.pallas_call(functools.partial(reduce_kernel, n_mp, chunk, gather), out...  84.6 us
    all_gather x1, waiting for transfers between devices, body(): full_down = lax.all_gather(w_down, 'dp', axis=1, tiled=True)  22.7 us
    unnamed x31, local copies, waits for them, and re-layouts  17.9 us
  transfers between devices with their start and end apart: 2, of which 1 were waited for; matrix products, arithmetic and copies ran while one was open for 4% of the time, Pallas kernels for 14%

profile of v2, /device:TPU:0, one launch (start us, length us, event | category | flops | bytes accessed | tf_op | source)
XLA Modules:
  0.0 443.8 jit_solution(12188120954295442501)
XLA Ops:
  7.2 0.0 all-gather.3.cloned.1.call-start
  7.2 0.7 fusion.1
  7.9 0.1 convert_reduce_fusion
  8.0 0.1 select_reduce_fusion.3
  8.1 0.1 sub.11
  8.2 0.1 copy.22
  8.3 0.9 copy.23
  9.3 0.6 pad_add_fusion.1.table
  9.9 33.8 %pick.3 = bf16[16,32,1024]{2,1,0:T(8,128)(2,1)} custom-call(s32[17]{0:T(128)} %pad_add_fusion.1.table, bf16[14,4,32,1024]{3,2,1,0:T(8,128)(2,1)} %bitcast.45), custom_call_target="tpu_custom_call" | custom-call | tf_op jit(solution)/shard_map/pick/pallas_call | solution.py:182
  43.7 0.0 copy-done.12
  43.7 0.0 copy-done.11
  43.7 0.1 select_reduce_fusion.1
  43.8 0.1 broadcast_in_dim.100
  43.9 0.6 pad_add_fusion.refs_1_
  44.5 0.0 copy-done.8
  44.5 0.0 copy-done.9
  44.5 0.0 copy-done.10
  44.5 0.7 pad_maximum_fusion.1.refs_2_
  45.3 66.9 %swap_1.1 = (bf16[8,2,4,32,1024]{4,3,2,1,0:T(8,128)(2,1)}, s32[8,2,8,128]{3,2,1,0:T(8,128)}, bf16[8,128,1024]{2,1,0:T(8,128)(2,1)}) custom-call(bf16[8,2,32,1024]{3,2,1,0:T(8,128)(2,1)} %bitcast.42, s32[8,2,8,128]{3,2,1,0:T(8,128)} %pad_add_fusion.refs_1_, bf16[128,1024]{1,0:T(8,128)(2,1)} %pad_maximum_fusion.1.refs_2_), custom_call_target="tpu_custom_call" | custom-call | tf_op jit(solution)/shard_map/swap_1/pallas_call | solution.py:154
  112.2 0.0 all-gather.3.cloned.1.call-update
  112.2 0.0 all-gather.5.cloned.1.call-start
  112.3 0.7 all-gather.5.cloned.1.call-update
  113.0 0.8 slice.12
  113.8 0.8 slice.13
  114.7 0.1 copy.27
  114.8 0.1 select_reduce_fusion
  114.9 0.3 copy.29
  115.2 1.1 slice.14.refs_5_
  116.3 0.1 select_reduce_fusion.2
  116.4 0.1 pad_add_fusion.2.table
  116.5 6.9 %project.1 = (bf16[14,32,1024]{2,1,0:T(8,128)(2,1)S(1)}, bf16[1792,256]{1,0:T(8,128)(2,1)S(1)}, bf16[1792,256]{1,0:T(8,128)(2,1)S(1)}, bf16[1792,256]{1,0:T(8,128)(2,1)S(1)}) custom-call(s32[15]{0:T(128)S(1)} %pad_add_fusion.2.table, bf16[16,4,32,1024]{3,2,1,0:T(8,128)(2,1)} %bitcast.44, bf16[1024,1024]{1,0:T(8,128)(2,1)S(1)} %bitcast.34), custom_call_target="tpu_custom_call" | custom-call | tf_op jit(solution)/shard_map/project/pallas_call | solution.py:232
  123.4 0.2 pad_maximum_fusion
  123.6 0.0 copy-start.4
  123.6 0.0 copy-start.5
  123.6 12.4 %copy.26 = bf16[1792,2,256]{2,1,0:T(2,128)(2,1)} copy(bf16[1792,2,256]{2,0,1:T(8,128)(2,1)S(1)} %pad_maximum_fusion) | data formatting | bytes 3670016
  136.0 0.0 copy-done.5
  136.0 56.6 %reduce_2.1.refs_0_.refs_3_ = bf16[14,4,32,1024]{3,2,1,0:T(8,128)(2,1)} custom-call(bf16[1792,256]{1,0:T(8,128)(2,1)S(1)} %get-tuple-element.16.refs_0_, bf16[1792,256]{1,0:T(8,128)(2,1)S(1)} %get-tuple-element.17.refs_1_, bf16[1792,256]{1,0:T(8,128)(2,1)S(1)} %get-tuple-element.18.refs_2_, s32[1792,1]{1,0:T(8,128)S(1)} %bitcast.32, s32[1,1792]{1,0:T(1,128)S(1)} %bitcast.36, ...), custom_call_target="tpu_custom_call" | custom-call | tf_op jit(solution)/shard_map/reduce_2/pallas_call | solution.py:417
  192.7 0.5 broadcast_maximum_fusion.table
  193.2 22.7 %all-gather.5.cloned.1.call-done.refs_2_ = bf16[1024,1024]{1,0:T(8,128)(2,1)} async-done(((bf16[1024,128]{1,0:T(8,128)(2,1)}), bf16[1024,1024]{1,0:T(8,128)(2,1)}) %all-gather.5.cloned.1.call-update) | async-done | bytes 2097168 | tf_op jit(solution)/shard_map/all_gather | solution.py:486
  215.9 0.0 copy-done.7
  215.9 1.6 copy-done.2
  217.5 1.6 copy-done.3
  219.1 28.0 %reduce_3.1.src = bf16[14,32,1024]{2,1,0:T(8,128)(2,1)S(1)} custom-call(bf16[14,4,32,1024]{3,2,1,0:T(8,128)(2,1)} %reduce_2.1.refs_0_.refs_3_, bf16[1024,1024]{1,0:T(8,128)(2,1)S(1)} %copy-done.2, bf16[1024,1024]{1,0:T(8,128)(2,1)S(1)} %copy-done.3, bf16[14,4,32,1024]{3,2,1,0:T(8,128)(2,1)} %reduce_2.1.refs_0_.refs_3_, f32[1,1,1024]{2,1,0:T(1,128)S(1)} %bitcast.39, ...), custom_call_target="tpu_custom_call" | custom-call | tf_op jit(solution)/shard_map/reduce_3/pallas_call | solution.py:417
  247.1 0.0 copy-start
  247.1 0.9 copy-done
  248.0 33.7 %pick.4 = bf16[16,32,1024]{2,1,0:T(8,128)(2,1)} custom-call(s32[16]{0:T(128)} %broadcast_maximum_fusion.table, bf16[14,32,1024]{2,1,0:T(8,128)(2,1)} %copy-done), custom_call_target="tpu_custom_call" | custom-call | tf_op jit(solution)/shard_map/pick/pallas_call | solution.py:182
  281.7 42.2 %swap_4.1 = bf16[8,2,4,32,1024]{4,3,2,1,0:T(8,128)(2,1)} custom-call(bf16[8,2,32,1024]{3,2,1,0:T(8,128)(2,1)} %bitcast.43), custom_call_target="tpu_custom_call" | custom-call | tf_op jit(solution)/shard_map/swap_4/pallas_call | solution.py:154
  323.8 113.1 %pick.5 = bf16[14,128,1024]{2,1,0:T(8,128)(2,1)} custom-call(s32[14]{0:T(128)} %copy-done.12, bf16[16,128,1024]{2,1,0:T(8,128)(2,1)} %bitcast.41), custom_call_target="tpu_custom_call" | custom-call | tf_op jit(solution)/shard_map/pick/pallas_call | solution.py:182
  (19 shorter events, 0.1 us)
Async XLA Ops:
  7.2 186.0 %all-gather.3.cloned.1.call-start = ((), (), s32[]{:S(2)}) async-start(), calls=%async_computation | async-start | bytes 2359296 | tf_op jit(solution)/shard_map/all_gather | solution.py:485
  8.0 35.7 %copy-start.12 = (s32[14]{0:T(128)}, s32[14]{0:T(128)S(1)}, u32[]{:S(2)}) copy-start(s32[14]{0:T(128)S(1)} %multiply_add_fusion.table) | copy-start | bytes 172
  9.8 33.8 %copy-start.11 = (s32[1792]{0:T(1024)S(1)}, s32[1792]{0:T(1024)}, u32[]{:S(2)}) copy-start(s32[1792]{0:T(1024)} %param.14) | copy-start | bytes 21508
  9.8 34.7 %copy-start.8 = (bf16[128,256]{1,0:T(8,128)(2,1)S(1)}, bf16[128,256]{1,0:T(8,128)(2,1)}, u32[]{:S(2)}) copy-start(bf16[128,256]{1,0:T(8,128)(2,1)} %param.18) | copy-start | bytes 196612
  9.9 34.7 %copy-start.9 = (bf16[128,256]{1,0:T(8,128)(2,1)S(1)}, bf16[128,256]{1,0:T(8,128)(2,1)}, u32[]{:S(2)}) copy-start(bf16[128,256]{1,0:T(8,128)(2,1)} %param.17) | copy-start | bytes 196612
  9.9 34.7 %copy-start.10 = (bf16[128,256]{1,0:T(8,128)(2,1)S(1)}, bf16[128,256]{1,0:T(8,128)(2,1)}, u32[]{:S(2)}) copy-start(bf16[128,256]{1,0:T(8,128)(2,1)} %param.16) | copy-start | bytes 196612
  112.2 4.3 copy-start.1
  112.2 103.7 %all-gather.5.cloned.1.call-start = ((), (), s32[]{:S(2)}) async-start(), calls=%async_computation.1 | async-start | bytes 2359296 | tf_op jit(solution)/shard_map/all_gather | solution.py:486
  123.6 12.4 %copy-start.4 = (f32[1024]{0:T(1024)S(1)}, f32[1024]{0:T(1024)}, u32[]{:S(2)}) copy-start(f32[1024]{0:T(1024)} %param.22) | copy-start | bytes 12292
  123.6 12.4 %copy-start.5 = (f32[1024]{0:T(1024)S(1)}, f32[1024]{0:T(1024)}, u32[]{:S(2)}) copy-start(f32[1024]{0:T(1024)} %param.23) | copy-start | bytes 12292
  136.0 79.9 %copy-start.6 = (f32[1024]{0:T(1024)S(1)}, f32[1024]{0:T(1024)}, u32[]{:S(2)}) copy-start(f32[1024]{0:T(1024)} %param.24) | copy-start | bytes 12292
  136.0 79.9 %copy-start.7 = (f32[1024]{0:T(1024)S(1)}, f32[1024]{0:T(1024)}, u32[]{:S(2)}) copy-start(f32[1024]{0:T(1024)} %param.25) | copy-start | bytes 12292
  215.9 1.6 copy-start.2
  217.5 1.6 copy-start.3
  247.1 0.9 copy-start
Sparse Core Ops, SparseCore 0:
  112.3 52.1 all-gather.2
  166.5 49.3 all-gather.4
